TPU v7x, 256 devices: a whole 4x4x8 slice. The times are simulated.
256 devices in a mesh: dp: 32 (over z, y_hi, core), mp: 8 (over x, y_lo).
Axes of the slice: x: 4, y: 4 (y_hi: 2, y_lo: 2; y = y_hi * 2 + y_lo), z: 8, core: 2. Of those that a mesh axis runs over, the one named last changes fastest.
Arguments:
- queries: bfloat16 [512, 4, 12288], P('dp', None, 'mp'), may hold values from -14 to 14
- new_keys: bfloat16 [512, 4, 1024], P('dp', None, 'mp'), may hold values from -13 to 13
- new_values: bfloat16 [512, 4, 1024], P('dp', None, 'mp'), may hold values from -24 to 24
- key_cache: bfloat16 [512, 8, 128, 128], P('dp', 'mp'), may hold values from -13 to 13
- value_cache: bfloat16 [512, 8, 128, 128], P('dp', 'mp'), may hold values from -24 to 24
- key_spill: bfloat16 [512, 8, 128, 128], P('dp', 'mp'), may hold values from -13 to 13
- value_spill: bfloat16 [512, 8, 128, 128], P('dp', 'mp'), may hold values from -24 to 24
- lengths: int32 [512], replicated, may hold values from 2 to 256, as said below
- partner: int32 [32], replicated, may hold values from 0 to 31, as said below
- out_weight: bfloat16 [12288, 12288], P('mp', 'dp'), may hold values from -0.0546875 to 0.0546875
Outputs:
- attention_out: bfloat16 [2048, 12288], P('mp', 'dp')
Inputs may be any that keep to these rules, and one draw needn't show every extreme that they name: partner[i] = i XOR 2**b for a single b of 0 to log2(32) - 1 chosen by the draw, so partner pairs the indices of dp and has no fixed point. `lengths`: some row has exactly 256 positions in every draw; the mean length differs from one index of dp to another.
All inputs are finite; a program needn't handle non-finite values.
Results may differ from a plain program's by a relative error of at most 0.0053.
Values may be sent and summed in bfloat16 or wider, within the bound.
A program may use at most 64 MiB of HBM per device.

v0:
```python
import functools
import math

import jax
import jax.numpy as jnp
from jax import lax
from jax.experimental import pallas as pl
from jax.experimental.pallas import tpu as pltpu
from jax.sharding import PartitionSpec as P

MESH = pl.DeviceIdType.MESH
MASKED = -1e30
F32, BF16 = jnp.float32, jnp.bfloat16

ROWS = 16
STEPS = 4
GROUP = 12
HEAD = 128
CAP = 128
COLS = GROUP * HEAD
OUT_COLS = 384
ROUNDS = 4
RPR = ROWS // ROUNDS
RB = RPR * STEPS
QR = GROUP * STEPS
QB = RPR * QR
Z, X = 8, 4
PIECES = ((0, 256), (256, 128))
SCALE2 = math.log2(math.e) / math.sqrt(HEAD)


def kernel(
    bit,
    lengths_hbm, q_hbm, nk_hbm, nv_hbm, k_hbm, v_hbm, sk_hbm, sv_hbm, w_hbm,
    out,
    lengths, q_own, nk, nv, k, v, sk, sv, w, w_far, q_far, o_own, m_own, l_own,
    t_send, st_send, t_recv, st_recv, g, ps, px, py_send, py, pf, po,
    load_sem, q_ss, q_rs, t_ss, t_rs, st_ss, st_rs, w_ss, w_rs, z_ss, c_ss, g_rs,
    px_ss, px_rs, py_ss, py_rs, po_ss, po_rs,
):
    me, mp = lax.axis_index("dp"), lax.axis_index("mp")
    z, yh, c = me // 4, (me // 2) % 2, me % 2
    x, yl = mp // 2, mp % 2
    mask = 2**bit
    partner = me + mask * (1 - 2 * ((me // mask) % 2))

    def plane(d):
        return lax.rem(z + d + Z, Z)

    def along_z(d):
        return {"dp": plane(d) * 4 + yh * 2 + c, "mp": mp}

    def along_y(hi, lo):
        return {"dp": z * 4 + hi * 2 + c, "mp": x * 2 + lo}

    far = {"dp": partner, "mp": mp}
    sibling = {"dp": z * 4 + yh * 2 + 1 - c, "mp": mp}

    loads = [
        pltpu.make_async_copy(src, dst, load_sem.at[i])
        for i, (src, dst) in enumerate(
            [
                (q_hbm, q_own), (lengths_hbm, lengths), (nk_hbm, nk), (nv_hbm, nv), (k_hbm, k), (v_hbm, v),
                (sk_hbm, sk), (sv_hbm, sv), (w_hbm, w),
            ]
        )
    ]
    for load in loads:
        load.start()

    barrier = pltpu.get_barrier_semaphore()
    peers = [{"dp": me, "mp": lax.rem(x + j, X) * 2 + yl} for j in range(1, X)]
    peers += [{"dp": z * 4 + (1 - yh) * 2 + c, "mp": j} for j in range(2 * X)]
    greeted = [along_z(d) for d in (1, -1, 2, -2)] + [sibling, far, along_y(yh, 1 - yl)] + peers
    for device in greeted:
        pl.semaphore_signal(barrier, inc=1, device_id=device, device_id_type=MESH)
    pl.semaphore_wait(barrier, len(greeted))

    def remote(src, dst, send_sem, recv_sem, device):
        return pltpu.make_async_remote_copy(
            src_ref=src, dst_ref=dst, send_sem=send_sem, recv_sem=recv_sem,
            device_id=device, device_id_type=MESH,
        )

    def q_copy(s):
        return remote(q_hbm.at[s], q_far.at[s], q_ss.at[s], q_rs.at[s], far)

    def t_copy(s):
        return remote(t_send.at[s], t_recv.at[s], t_ss.at[s], t_rs.at[s], far)

    def st_copy(s):
        return remote(st_send.at[s], st_recv.at[s], st_ss.at[s], st_rs.at[s], far)

    def w_copy(i):
        columns = pl.ds(*PIECES[i // 4])
        rows = pl.ds(0, COLS) if i == 4 else pl.ds(i * (COLS // 4), COLS // 4)
        return remote(
            w_hbm.at[rows, columns], w_far.at[rows, columns], w_ss.at[i], w_rs.at[i], along_y(1 - yh, yl)
        )

    for s in range(ROUNDS):
        q_copy(s).start()
    if bit != 1:
        for i in range(4):
            w_copy(i).start()
    for load in loads:
        load.wait()

    lane = lax.broadcasted_iota(jnp.int32, (1, CAP), 1)

    def bias_of(owner, s, less):
        return jnp.stack(
            [
                jnp.where(lane < lengths[owner * ROWS + s * RPR + r] - less, 0.0, MASKED)
                for r in range(RPR)
            ]
        )

    def scores_of(queries, keys, bias):
        raw = jnp.einsum("rqd,rkd->rqk", queries, keys, preferred_element_type=F32)
        return raw * SCALE2 + bias

    def own(s):
        q_row = lax.broadcasted_iota(jnp.int32, (QB, RB), 0)
        f_col = lax.broadcasted_iota(jnp.int32, (QB, RB), 1)
        first = (f_col >> 2) * QR
        fresh_ok = (q_row >= first) & (q_row < first + QR) & ((f_col & 3) <= (q_row & 3))
        fresh_bias = jnp.where(fresh_ok, 0.0, MASKED)
        rows = pl.ds(s * RPR, RPR)
        queries = q_own[s]
        cached = scores_of(queries.reshape(RPR, QR, HEAD), k[rows], bias_of(me, s, 0))
        fresh = lax.dot_general(
            queries, nk[s], (((1,), (1,)), ((), ())), preferred_element_type=F32
        )
        fresh = (fresh * SCALE2 + fresh_bias).reshape(RPR, QR, RB)
        peak = jnp.maximum(
            jnp.max(cached, axis=-1, keepdims=True), jnp.max(fresh, axis=-1, keepdims=True)
        )
        cached, fresh = jnp.exp2(cached - peak), jnp.exp2(fresh - peak)
        m_own[s] = peak
        l_own[s] = jnp.sum(cached, axis=-1, keepdims=True) + jnp.sum(fresh, axis=-1, keepdims=True)
        summed = jnp.einsum("rqk,rkd->rqd", cached.astype(BF16), v[rows], preferred_element_type=F32)
        o_own[s] = summed + jnp.dot(
            fresh.astype(BF16).reshape(QB, RB), nv[s], preferred_element_type=F32
        ).reshape(RPR, QR, HEAD)

    def diagonal():
        shape = (RPR, QR, CAP)
        return lax.broadcasted_iota(jnp.int32, shape, 1) == lax.broadcasted_iota(jnp.int32, shape, 2)

    def tail(s):
        rows = pl.ds(s * RPR, RPR)
        q_copy(s).wait_recv()
        scores = scores_of(q_far[s].reshape(RPR, QR, HEAD), sk[rows], bias_of(partner, s, CAP))
        peak = jnp.max(scores, axis=-1, keepdims=True)
        scores = jnp.exp2(scores - peak)
        weight = jnp.sum(scores, axis=-1, keepdims=True)
        summed = jnp.einsum("rqk,rkd->rqd", scores.astype(BF16), sv[rows], preferred_element_type=F32)
        t_send[s] = (summed / weight).astype(BF16).reshape(QB, HEAD)
        t_copy(s).start()
        st_send[s, 0:RPR] = jnp.sum(jnp.where(diagonal(), peak + jnp.log2(weight), 0.0), axis=1)
        st_copy(s).start()

        for i in range(ROUNDS):

            @pl.when(s == i)
            def _():
                if bit == 1:
                    w_copy(i).start()
                if i == ROUNDS - 1:
                    w_copy(4).start()

    def along(s, zz, d):
        ref = g.at[s, zz, c]
        return remote(ref, ref, z_ss.at[s, zz, d + 2], g_rs.at[s, zz, c], along_z(d))

    def to_core(s, zz):
        ref = g.at[s, zz, c]
        return remote(ref, ref, c_ss.at[s, zz], g_rs.at[s, zz, c], sibling)

    def arrived(s, zz, cc):
        ref = g.at[s, zz, cc]
        remote(ref, ref, c_ss.at[s, zz], g_rs.at[s, zz, cc], sibling).wait_recv()

    def merge(s):
        t_copy(s).wait_recv()
        st_copy(s).wait_recv()
        log_sum = jnp.sum(
            jnp.where(diagonal(), st_recv[s, 0:RPR][:, None, :], 0.0), axis=-1, keepdims=True
        )
        peak = jnp.maximum(m_own[s], log_sum)
        near_factor, far_factor = jnp.exp2(m_own[s] - peak), jnp.exp2(log_sum - peak)
        far_part = t_recv[s].reshape(RPR, QR, HEAD).astype(F32)
        total = near_factor * o_own[s] + far_factor * far_part
        context = (total / (near_factor * l_own[s] + far_factor)).astype(BF16)
        index = lax.broadcasted_iota(jnp.int32, (QB, QB), 0)
        source = ((index >> 2) & 3) * QR + (index >> 4) * STEPS + (index & 3)
        one_hot = jnp.where(lax.broadcasted_iota(jnp.int32, (QB, QB), 1) == source, 1.0, 0.0)
        heads = jnp.dot(
            one_hot.astype(BF16), context.reshape(QB, HEAD), preferred_element_type=F32
        ).astype(BF16)
        for h in range(GROUP):
            g[s, z, c, :, h * HEAD : (h + 1) * HEAD] = heads[h * RB : (h + 1) * RB]
        for d in (1, -1):
            along(s, z, d).start()
        to_core(s, z).start()

    def ring(s, d):
        for zz, away in ((plane(-d), 1), (plane(d), -1)):
            arrived(s, zz, c)
            if d < 3:
                along(s, zz, away).start()
            if d == 2:

                @pl.when(lax.rem(s, 2) == (1 - away) // 2)
                def _():
                    along(s, zz, 2 * away).start()

            to_core(s, zz).start()
        if d == 3:
            arrived(s, plane(4), c)
            to_core(s, plane(4)).start()

    def px_copy(s, zz):
        device = {"dp": me, "mp": (zz // 2) * 2 + yl}
        return remote(
            ps.at[s, zz], px.at[s, zz % 2, x], px_ss.at[s, zz], px_rs.at[s, zz % 2, x], device
        )

    def py_copy(s):
        return remote(py_send.at[s], py.at[s], py_ss.at[s], py_rs.at[s], along_y(yh, 1 - yl))

    def po_copy(s, zz, i):
        device = {"dp": z * 4 + (1 - yh) * 2 + c, "mp": zz}
        columns = pl.ds(*PIECES[i])
        return remote(
            pf.at[s, zz, :, columns], po.at[s, mp, :, columns], po_ss.at[s, zz, i], po_rs.at[s, mp, i], device
        )

    def product(s, distances, weight):
        planes = [plane(d) for d in distances]
        rows = jnp.concatenate([g[s, zz].reshape(2 * RB, COLS) for zz in planes], axis=0)
        whole = jnp.dot(rows, weight, preferred_element_type=F32).astype(BF16)
        return [(zz, whole[i * 2 * RB : (i + 1) * 2 * RB]) for i, zz in enumerate(planes)]

    def project(s, distances):
        for d in distances:
            arrived(s, plane(d), 1 - c)
        for zz, part in product(s, distances, w[...]):

            @pl.when(zz // 2 != x)
            def _():
                ps[s, zz] = part
                px_copy(s, zz).start()

            @pl.when(zz // 2 == x)
            def _():
                px[s, zz % 2, x] = part

    def project_far(s, distances, i):
        start, size = PIECES[i]
        for zz, part in product(s, distances, w_far[:, start : start + size]):
            pf[s, zz, :, start : start + size] = part
            po_copy(s, zz, i).start()

    def sum_x(s, lo):
        for j in range(X):

            @pl.when(x != j)
            def _():
                ref, sem = px.at[s, lo, j], px_rs.at[s, lo, j]
                remote(ref, ref, px_ss.at[s, 0], sem, sibling).wait_recv()

        total = px[s, lo, 0].astype(F32)
        for j in range(1, X):
            total = total + px[s, lo, j].astype(F32)
        return total

    def store(s, hi, total):
        for i in range(2):
            start = (hi * 2 + i) * ROWS * STEPS + s * RB
            out[pl.ds(pl.multiple_of(start, RB), RB), :] = total[i * RB : (i + 1) * RB].astype(BF16)

    def hand_over(s):
        py_send[s] = sum_x(s, 1 - yl).astype(BF16)
        py_copy(s).start()

    def finish(s):
        total = sum_x(s, yl)
        py_copy(s).wait_recv()
        store(s, yh, total + py[s].astype(F32))

    def finish_far(s, carry):
        for i in range(2):
            for j in range(2 * X):
                ref, sem = po.at[s, j, :, pl.ds(*PIECES[i])], po_rs.at[s, j, i]
                remote(ref, ref, po_ss.at[s, 0, i], sem, sibling).wait_recv()
        total = po[s, 0].astype(F32)
        for j in range(1, 2 * X):
            total = total + po[s, j].astype(F32)
        store(s, 1 - yh, total)
        return carry

    inner, outer = (0, -1, 1, -2, 2), (-3, 3, 4)
    last = ROUNDS - 1
    stages = [
        (0, own), (0, tail), (1, merge),
        *[(1 + d, functools.partial(ring, d=d)) for d in (1, 2, 3)],
        (4, functools.partial(project, distances=outer)),
        (3, functools.partial(project, distances=inner)),
        (5, hand_over), (6, finish),
    ]

    def slot(t, carry):
        for behind, stage in stages:
            s = t - behind

            @pl.when((s >= 0) & (s < ROUNDS))
            def _():
                stage(s)

        @pl.when(t == 4)
        def _():
            for i in range(4):
                w_copy(i).wait_recv()

        @pl.when((t >= 4) & (t < 4 + last))
        def _():
            project_far(t - 4, inner + outer, 0)

        @pl.when(t == 3 + last)
        def _():
            project_far(last, inner, 0)
            w_copy(4).wait_recv()

        @pl.when(t == 4 + last)
        def _():
            project_far(last, outer, 0)

        @pl.when((t == 3 + last) | (t == 4 + last))
        def _():
            def second(s, carry):
                project_far(s, inner + outer, 1)
                return carry

            late = t - 3 - last
            lax.fori_loop(late * last, last + late, second, 0)

        return carry

    lax.fori_loop(0, ROUNDS + max(behind for behind, _ in stages), slot, 0)
    lax.fori_loop(0, ROUNDS, finish_far, 0)

    def drain(s, carry):
        q_copy(s).wait_send()
        t_copy(s).wait_send()
        st_copy(s).wait_send()
        for away in (1, -1):
            for d in range(3):
                along(s, plane(-d * away), away).wait_send()

            @pl.when(lax.rem(s, 2) == (1 - away) // 2)
            def _():
                along(s, plane(-2 * away), 2 * away).wait_send()

        py_copy(s).wait_send()
        for zz in range(Z):
            to_core(s, zz).wait_send()
            for i in range(2):
                po_copy(s, zz, i).wait_send()

            @pl.when(zz // 2 != x)
            def _():
                px_copy(s, zz).wait_send()

        return carry

    lax.fori_loop(0, ROUNDS, drain, 0)
    for i in range(5):
        w_copy(i).wait_send()


def attention(bit, *arrays):
    any_space = pl.BlockSpec(memory_space=pl.ANY)
    dma = pltpu.SemaphoreType.DMA
    return pl.pallas_call(
        functools.partial(kernel, bit),
        name=f"attention_{bit}",
        out_shape=jax.ShapeDtypeStruct((4 * ROWS * STEPS, OUT_COLS), BF16),
        in_specs=[any_space] * 9,
        out_specs=pl.BlockSpec(memory_space=pltpu.VMEM),
        scratch_shapes=[
            pltpu.SMEM((ROWS * 32,), jnp.int32),
            pltpu.VMEM((ROUNDS, QB, HEAD), BF16),
            *[pltpu.VMEM((ROUNDS, RB, HEAD), BF16)] * 2,
            *[pltpu.VMEM((ROWS, CAP, HEAD), BF16)] * 4,
            *[pltpu.VMEM((COLS, OUT_COLS), BF16)] * 2,
            pltpu.VMEM((ROUNDS, QB, HEAD), BF16),
            pltpu.VMEM((ROUNDS, RPR, QR, HEAD), F32),
            pltpu.VMEM((ROUNDS, RPR, QR, 1), F32),
            pltpu.VMEM((ROUNDS, RPR, QR, 1), F32),
            pltpu.VMEM((ROUNDS, QB, HEAD), BF16),
            pltpu.VMEM((ROUNDS, 8, HEAD), F32),
            pltpu.VMEM((ROUNDS, QB, HEAD), BF16),
            pltpu.VMEM((ROUNDS, 8, HEAD), F32),
            pltpu.VMEM((ROUNDS, Z, 2, RB, COLS), BF16),
            pltpu.VMEM((ROUNDS, Z, 2 * RB, OUT_COLS), BF16),
            pltpu.VMEM((ROUNDS, 2, X, 2 * RB, OUT_COLS), BF16),
            pltpu.VMEM((ROUNDS, 2 * RB, OUT_COLS), BF16),
            pltpu.VMEM((ROUNDS, 2 * RB, OUT_COLS), BF16),
            pltpu.VMEM((ROUNDS, Z, 2 * RB, OUT_COLS), BF16),
            pltpu.VMEM((ROUNDS, 2 * X, 2 * RB, OUT_COLS), BF16),
            dma((9,)),
            *[dma((ROUNDS,))] * 6,
            *[dma((5,))] * 2,
            dma((ROUNDS, Z, 5)),
            dma((ROUNDS, Z)),
            dma((ROUNDS, Z, 2)),
            dma((ROUNDS, Z)),
            dma((ROUNDS, 2, X)),
            *[dma((ROUNDS,))] * 2,
            *[dma((ROUNDS, Z, 2))] * 2,
        ],
        compiler_params=pltpu.CompilerParams(
            collective_id=bit + 1, has_side_effects=True, vmem_limit_bytes=48 << 20
        ),
    )(*arrays)


def body(
    queries, new_keys, new_values, key_cache, value_cache, key_spill, value_spill,
    lengths, partner, out_weight,
):
    by_head = queries.reshape(ROWS, STEPS, GROUP, HEAD).transpose(0, 2, 1, 3)
    arrays = (
        lengths,
        by_head.reshape(ROUNDS, QB, HEAD),
        new_keys.reshape(ROUNDS, RB, HEAD),
        new_values.reshape(ROUNDS, RB, HEAD),
        *[a.reshape(ROWS, CAP, HEAD) for a in (key_cache, value_cache, key_spill, value_spill)],
        out_weight,
    )
    levels = lax.axis_size("dp").bit_length() - 1
    bit = 31 - lax.clz(partner[0])
    return lax.switch(bit, [functools.partial(attention, b) for b in range(levels)], *arrays)


def solution(mesh):
    return jax.shard_map(
        body,
        mesh=mesh,
        in_specs=(
            P("dp", None, "mp"),
            P("dp", None, "mp"),
            P("dp", None, "mp"),
            P("dp", "mp", None, None),
            P("dp", "mp", None, None),
            P("dp", "mp", None, None),
            P("dp", "mp", None, None),
            P(),
            P(),
            P("mp", "dp"),
        ),
        out_specs=P("mp", "dp"),
        check_vma=False,
    )
```

profile of v0, /device:TPU:1, one launch (start us, length us, event | category | flops | bytes accessed | tf_op | source)
XLA Modules:
  0.0 60.4 jit_solution(5981522174134814052)
XLA Ops:
  0.7 59.1 %conditional.1 = (bf16[256,384]{1,0:T(8,128)(2,1)S(1)}) conditional(s32[]{:T(128)} %bitcast.55, (s32[512]{0:T(512)}, bf16[16,12,4,128]{3,2,1,0:T(4,128)(2,1)}, bf16[16,4,128]{2,1,0:T(4,128)(2,1)}, bf16[16,4,128]{2,1,0:T(4,128)(2,1)}, bf16[16,1,128,128]{3,2,1,0:T(8,128)(2,1)}, ...), branch_computations={%region_0.0_spmd, %region_1.0_spmd, %region_2.0_spmd, %region_3.0_... | conditional | bytes 8 | solution.py:445
  0.7 58.8 %attention_0.1 = bf16[256,384]{1,0:T(8,128)(2,1)S(1)} custom-call(s32[512]{0:T(512)} %get-tuple-element.192.lengths_hbm, bf16[4,192,128]{2,1,0:T(8,128)(2,1)} %bitcast.85, bf16[4,16,128]{2,1,0:T(8,128)(2,1)} %bitcast.90, bf16[4,16,128]{2,1,0:T(8,128)(2,1)} %bitcast.95, bf16[16,128,128]{2,1,0:T(8,128)(2,1)} %bitcast.60, bf16[16,128,128]{2,1,0:T(8,128)(2,1)} %bitcast.65, ...), custom_call_target="tpu_custom_call" | custom-call | tf_op jit(solution)/shard_map/cond/branch_0_fun/attention_0/pallas_call | solution.py:386
  59.8 0.7 %copy.82 = bf16[256,384]{1,0:T(8,128)(2,1)} copy(bf16[256,384]{1,0:T(8,128)(2,1)S(1)} %get-tuple-element.146) | data formatting | bytes 393216
where the time goes:
time: 60.5 us; the launch traced here: 60.4 us
  Pallas kernels  58.8 us (97%)
  local copies, waits for them, and re-layouts  0.68 us (1%)
  between operations  0.66 us (1%)
    pallas_call x1, Pallas kernels, attention(): pl.pallas_call(functools.partial(kernel, bit), name=f'attention_{bit}', o...  58.8 us

commit v1 on v0

--- a/solution.py
+++ b/solution.py
@@ -25,7 +25,10 @@
 QR = GROUP * STEPS
 QB = RPR * QR
 Z, X = 8, 4
-PIECES = ((0, 256), (256, 128))
+PIECES = ((0, OUT_COLS), (OUT_COLS, 256), (OUT_COLS + 256, 128))
+LAST = ROUNDS - 1
+LAG = (1, 1, 1, 2, 2)
+HANDED = ((0, OUT_COLS), (0, 256), (256, 128))
 SCALE2 = math.log2(math.e) / math.sqrt(HEAD)
 
 
@@ -34,9 +37,9 @@
     lengths_hbm, q_hbm, nk_hbm, nv_hbm, k_hbm, v_hbm, sk_hbm, sv_hbm, w_hbm,
     out,
     lengths, q_own, nk, nv, k, v, sk, sv, w, w_far, q_far, o_own, m_own, l_own,
-    t_send, st_send, t_recv, st_recv, g, ps, px, py_send, py, pf, po,
-    load_sem, q_ss, q_rs, t_ss, t_rs, st_ss, st_rs, w_ss, w_rs, z_ss, c_ss, g_rs,
-    px_ss, px_rs, py_ss, py_rs, po_ss, po_rs,
+    t_send, st_send, t_recv, st_recv, g, ps, px, py_send, py,
+    load_sem, q_ss, q_rs, t_ss, t_rs, st_ss, st_rs, w_ss, w_rs, z_ss, z_rs, c_ss, c_rs,
+    px_ss, px_rs, py_ss, py_rs,
 ):
     me, mp = lax.axis_index("dp"), lax.axis_index("mp")
     z, yh, c = me // 4, (me // 2) % 2, me % 2
@@ -70,8 +73,8 @@
 
     barrier = pltpu.get_barrier_semaphore()
     peers = [{"dp": me, "mp": lax.rem(x + j, X) * 2 + yl} for j in range(1, X)]
-    peers += [{"dp": z * 4 + (1 - yh) * 2 + c, "mp": j} for j in range(2 * X)]
-    greeted = [along_z(d) for d in (1, -1, 2, -2)] + [sibling, far, along_y(yh, 1 - yl)] + peers
+    column = [along_y(yh, 1 - yl), along_y(1 - yh, 0), along_y(1 - yh, 1)]
+    greeted = [along_z(d) for d in (1, -1, 2, -2)] + [sibling, far] + column + peers
     for device in greeted:
         pl.semaphore_signal(barrier, inc=1, device_id=device, device_id_type=MESH)
     pl.semaphore_wait(barrier, len(greeted))
@@ -92,7 +95,7 @@
         return remote(st_send.at[s], st_recv.at[s], st_ss.at[s], st_rs.at[s], far)
 
     def w_copy(i):
-        columns = pl.ds(*PIECES[i // 4])
+        columns = pl.ds(256, 128) if i == 4 else pl.ds(0, 256)
         rows = pl.ds(0, COLS) if i == 4 else pl.ds(i * (COLS // 4), COLS // 4)
         return remote(
             w_hbm.at[rows, columns], w_far.at[rows, columns], w_ss.at[i], w_rs.at[i], along_y(1 - yh, yl)
@@ -172,15 +175,11 @@
 
     def along(s, zz, d):
         ref = g.at[s, zz, c]
-        return remote(ref, ref, z_ss.at[s, zz, d + 2], g_rs.at[s, zz, c], along_z(d))
-
-    def to_core(s, zz):
+        return remote(ref, ref, z_ss.at[s], z_rs.at[s, zz], along_z(d))
+
+    def to_core(s, zz, half):
         ref = g.at[s, zz, c]
-        return remote(ref, ref, c_ss.at[s, zz], g_rs.at[s, zz, c], sibling)
-
-    def arrived(s, zz, cc):
-        ref = g.at[s, zz, cc]
-        remote(ref, ref, c_ss.at[s, zz], g_rs.at[s, zz, cc], sibling).wait_recv()
+        return remote(ref, ref, c_ss.at[s], c_rs.at[s, half], sibling)
 
     def merge(s):
         t_copy(s).wait_recv()
@@ -203,11 +202,12 @@
             g[s, z, c, :, h * HEAD : (h + 1) * HEAD] = heads[h * RB : (h + 1) * RB]
         for d in (1, -1):
             along(s, z, d).start()
-        to_core(s, z).start()
+
+        to_core(s, z, 0).start()
 
     def ring(s, d):
         for zz, away in ((plane(-d), 1), (plane(d), -1)):
-            arrived(s, zz, c)
+            along(s, zz, 1).wait_recv()
             if d < 3:
                 along(s, zz, away).start()
             if d == 2:
@@ -216,163 +216,177 @@
                 def _():
                     along(s, zz, 2 * away).start()
 
-            to_core(s, zz).start()
+            to_core(s, zz, d // 3).start()
         if d == 3:
-            arrived(s, plane(4), c)
-            to_core(s, plane(4)).start()
-
-    def px_copy(s, zz):
-        device = {"dp": me, "mp": (zz // 2) * 2 + yl}
-        return remote(
-            ps.at[s, zz], px.at[s, zz % 2, x], px_ss.at[s, zz], px_rs.at[s, zz % 2, x], device
-        )
-
-    def py_copy(s):
-        return remote(py_send.at[s], py.at[s], py_ss.at[s], py_rs.at[s], along_y(yh, 1 - yl))
-
-    def po_copy(s, zz, i):
-        device = {"dp": z * 4 + (1 - yh) * 2 + c, "mp": zz}
+            along(s, plane(4), 1).wait_recv()
+            to_core(s, plane(4), 1).start()
+
+    def px_copy(s, j, i):
         columns = pl.ds(*PIECES[i])
         return remote(
-            pf.at[s, zz, :, columns], po.at[s, mp, :, columns], po_ss.at[s, zz, i], po_rs.at[s, mp, i], device
-        )
-
-    def product(s, distances, weight):
+            ps.at[s, pl.ds(2 * j, 2), :, columns], px.at[s, x, :, :, columns],
+            px_ss.at[s, i], px_rs.at[s, i], {"dp": me, "mp": 2 * j + yl},
+        )
+
+    def px_arrived(s, i):
+        ref = px.at[s, pl.ds(0, X - 1), :, :, pl.ds(*PIECES[i])]
+        remote(ref, ref, px_ss.at[s, i], px_rs.at[s, i], sibling).wait_recv()
+
+    def py_copy(s, k, i):
+        device = along_y(1 - yh, k - 1) if k else along_y(yh, 1 - yl)
+        columns = pl.ds(*HANDED[i])
+        return remote(
+            py_send.at[s, k, :, columns], py.at[s, 1 + yl if k else 0, :, columns],
+            py_ss.at[s, i], py_rs.at[s, i], device,
+        )
+
+    def py_parts(ref, s, i):
+        return ref.at[s, pl.ds(1, 2) if i else 0, :, pl.ds(*HANDED[i])]
+
+    def project(s, weights, i):
+        rows = g[s].reshape(Z * 2 * RB, COLS)
+        start = PIECES[i][0]
+        for weight in weights:
+            product = jnp.dot(rows, weight, preferred_element_type=F32).astype(BF16)
+            columns = slice(start, start + weight.shape[1])
+            start += weight.shape[1]
+            product = product.reshape(Z, 2 * RB, weight.shape[1])
+            ps[s, :, :, columns] = product
+            for j in range(X):
+
+                @pl.when(x == j)
+                def _():
+                    px[s, j, :, :, columns] = product[2 * j : 2 * j + 2]
+
+        for j in range(X):
+
+            @pl.when(x != j)
+            def _():
+                px_copy(s, j, i).start()
+
+    inner, outer = (0, -1, 1, -2, 2), (-3, 3, 4)
+
+    def plane_copy(s, zz):
+        columns = pl.ds(*PIECES[0])
+        return remote(
+            ps.at[s, zz, :, columns], px.at[s, x, lax.rem(zz, 2), :, columns],
+            px_ss.at[s, 0], px_rs.at[s, 0], {"dp": me, "mp": (zz // 2) * 2 + yl},
+        )
+
+    def project_own(s, distances):
+        half = int(distances == outer)
+        ref = g.at[s, pl.ds(0, len(distances)), 1 - c]
+        remote(ref, ref, c_ss.at[s], c_rs.at[s, half], sibling).wait_recv()
         planes = [plane(d) for d in distances]
         rows = jnp.concatenate([g[s, zz].reshape(2 * RB, COLS) for zz in planes], axis=0)
-        whole = jnp.dot(rows, weight, preferred_element_type=F32).astype(BF16)
-        return [(zz, whole[i * 2 * RB : (i + 1) * 2 * RB]) for i, zz in enumerate(planes)]
-
-    def project(s, distances):
-        for d in distances:
-            arrived(s, plane(d), 1 - c)
-        for zz, part in product(s, distances, w[...]):
+        product = jnp.dot(rows, w[...], preferred_element_type=F32).astype(BF16)
+        for j, zz in enumerate(planes):
+            mine = product[j * 2 * RB : (j + 1) * 2 * RB]
 
             @pl.when(zz // 2 != x)
             def _():
-                ps[s, zz] = part
-                px_copy(s, zz).start()
+                ps[s, zz, :, :OUT_COLS] = mine
+                plane_copy(s, zz).start()
 
             @pl.when(zz // 2 == x)
             def _():
-                px[s, zz % 2, x] = part
-
-    def project_far(s, distances, i):
-        start, size = PIECES[i]
-        for zz, part in product(s, distances, w_far[:, start : start + size]):
-            pf[s, zz, :, start : start + size] = part
-            po_copy(s, zz, i).start()
-
-    def sum_x(s, lo):
-        for j in range(X):
-
-            @pl.when(x != j)
-            def _():
-                ref, sem = px.at[s, lo, j], px_rs.at[s, lo, j]
-                remote(ref, ref, px_ss.at[s, 0], sem, sibling).wait_recv()
-
-        total = px[s, lo, 0].astype(F32)
-        for j in range(1, X):
-            total = total + px[s, lo, j].astype(F32)
-        return total
-
-    def store(s, hi, total):
-        for i in range(2):
-            start = (hi * 2 + i) * ROWS * STEPS + s * RB
-            out[pl.ds(pl.multiple_of(start, RB), RB), :] = total[i * RB : (i + 1) * RB].astype(BF16)
-
-    def hand_over(s):
-        py_send[s] = sum_x(s, 1 - yl).astype(BF16)
-        py_copy(s).start()
-
-    def finish(s):
-        total = sum_x(s, yl)
-        py_copy(s).wait_recv()
-        store(s, yh, total + py[s].astype(F32))
-
-    def finish_far(s, carry):
-        for i in range(2):
-            for j in range(2 * X):
-                ref, sem = po.at[s, j, :, pl.ds(*PIECES[i])], po_rs.at[s, j, i]
-                remote(ref, ref, po_ss.at[s, 0, i], sem, sibling).wait_recv()
-        total = po[s, 0].astype(F32)
-        for j in range(1, 2 * X):
-            total = total + po[s, j].astype(F32)
-        store(s, 1 - yh, total)
-        return carry
-
-    inner, outer = (0, -1, 1, -2, 2), (-3, 3, 4)
-    last = ROUNDS - 1
-    stages = [
-        (0, own), (0, tail), (1, merge),
-        *[(1 + d, functools.partial(ring, d=d)) for d in (1, 2, 3)],
-        (4, functools.partial(project, distances=outer)),
-        (3, functools.partial(project, distances=inner)),
-        (5, hand_over), (6, finish),
-    ]
-
-    def slot(t, carry):
-        for behind, stage in stages:
-            s = t - behind
-
-            @pl.when((s >= 0) & (s < ROUNDS))
-            def _():
-                stage(s)
-
-        @pl.when(t == 4)
+                px[s, x, lax.rem(zz, 2), :, :OUT_COLS] = mine
+
+    def project_first(s):
+        @pl.when(s == 0)
         def _():
             for i in range(4):
                 w_copy(i).wait_recv()
 
-        @pl.when((t >= 4) & (t < 4 + last))
+        project(s, (w_far[:, :256],), 1)
+
+    def project_second(s):
+        @pl.when(s == 0)
         def _():
-            project_far(t - 4, inner + outer, 0)
-
-        @pl.when(t == 3 + last)
-        def _():
-            project_far(last, inner, 0)
             w_copy(4).wait_recv()
 
-        @pl.when(t == 4 + last)
-        def _():
-            project_far(last, outer, 0)
-
-        @pl.when((t == 3 + last) | (t == 4 + last))
-        def _():
-            def second(s, carry):
-                project_far(s, inner + outer, 1)
-                return carry
-
-            late = t - 3 - last
-            lax.fori_loop(late * last, last + late, second, 0)
+        project(s, (w_far[:, 256:],), 2)
+
+    def sum_x(s, lo, columns):
+        total = px[s, 0, lo, :, columns].astype(F32)
+        for j in range(1, X):
+            total = total + px[s, j, lo, :, columns].astype(F32)
+        return total
+
+    def hand_over(s, i):
+        start, size = HANDED[i]
+        offset = OUT_COLS if i else 0
+        for k in (1, 2) if i else (0,):
+            total = sum_x(s, k - 1 if k else 1 - yl, slice(offset + start, offset + start + size))
+            py_send[s, k, :, start : start + size] = total.astype(BF16)
+            py_copy(s, k, i).start()
+
+    def hand_first(s):
+        px_arrived(s, 0)
+        hand_over(s, 0)
+        px_arrived(s, 1)
+        hand_over(s, 1)
+
+    def hand_second(s):
+        px_arrived(s, 2)
+        hand_over(s, 2)
+
+    def finish(s):
+        for i in range(3):
+            ref = py_parts(py, s, i)
+            remote(ref, ref, py_ss.at[s, i], py_rs.at[s, i], sibling).wait_recv()
+        own_rows = sum_x(s, yl, slice(0, OUT_COLS)) + py[s, 0].astype(F32)
+        far_rows = py[s, 1].astype(F32) + py[s, 2].astype(F32)
+        for hi, total in ((yh, own_rows), (1 - yh, far_rows)):
+            for i in range(2):
+                start = (hi * 2 + i) * ROWS * STEPS + s * RB
+                part = total[i * RB : (i + 1) * RB].astype(BF16)
+                out[pl.ds(pl.multiple_of(start, RB), RB), :] = part
+
+    part, early = functools.partial, bit >= 3
+    stages = [(own, (0, 1, 2, 3)), (tail, (0, 1, 2, 3))] + [
+        (stage, tuple(at + LAG[bit] for at in slots))
+        for stage, slots in (
+            (merge, (0, 1, 2, 3)),
+            (part(ring, d=1), (1, 2, 3, 4)),
+            (part(ring, d=2), (2, 3, 4, 5)),
+            (part(ring, d=3), (3, 4, 5, 6)),
+            (part(project_own, distances=outer), (4, 5, 6, 6)),
+            (part(project_own, distances=inner), (3, 4, 5, 5)),
+            (project_first, (4, 5, 6, 6)),
+            (hand_first, (7, 7, 7, 7) if early else (6, 6, 7, 7)),
+            (project_second, (5, 5, 6, 6) if early else (6, 6, 6, 6)),
+            (hand_second, (7, 7, 7, 7)),
+            (finish, (8, 8, 8, 8)),
+        )
+    ]
+
+    def slot(t, carry):
+        for stage, slots in stages:
+
+            def one(s, inside, stage=stage):
+                stage(s)
+                return inside
+
+            begun = sum((t > at).astype(jnp.int32) for at in slots)
+            due = sum((t >= at).astype(jnp.int32) for at in slots)
+            lax.fori_loop(begun, due, one, 0)
 
         return carry
 
-    lax.fori_loop(0, ROUNDS + max(behind for behind, _ in stages), slot, 0)
-    lax.fori_loop(0, ROUNDS, finish_far, 0)
+    lax.fori_loop(0, 1 + max(slots[-1] for _, slots in stages), slot, 0)
 
     def drain(s, carry):
         q_copy(s).wait_send()
         t_copy(s).wait_send()
         st_copy(s).wait_send()
-        for away in (1, -1):
-            for d in range(3):
-                along(s, plane(-d * away), away).wait_send()
-
-            @pl.when(lax.rem(s, 2) == (1 - away) // 2)
-            def _():
-                along(s, plane(-2 * away), 2 * away).wait_send()
-
-        py_copy(s).wait_send()
-        for zz in range(Z):
-            to_core(s, zz).wait_send()
-            for i in range(2):
-                po_copy(s, zz, i).wait_send()
-
-            @pl.when(zz // 2 != x)
-            def _():
-                px_copy(s, zz).wait_send()
-
+        for ref, sem in (
+            (g.at[s, pl.ds(0, 7), 0], z_ss.at[s]),
+            (g.at[s, :, 0], c_ss.at[s]),
+            *[(ps.at[s, pl.ds(0, 2 * X - 2), :, pl.ds(*PIECES[i])], px_ss.at[s, i]) for i in range(3)],
+            *[(py_parts(py_send, s, i), py_ss.at[s, i]) for i in range(3)],
+        ):
+            remote(ref, ref, sem, c_rs.at[s, 0], sibling).wait_send()
         return carry
 
     lax.fori_loop(0, ROUNDS, drain, 0)
@@ -404,22 +418,19 @@
             pltpu.VMEM((ROUNDS, QB, HEAD), BF16),
             pltpu.VMEM((ROUNDS, 8, HEAD), F32),
             pltpu.VMEM((ROUNDS, Z, 2, RB, COLS), BF16),
-            pltpu.VMEM((ROUNDS, Z, 2 * RB, OUT_COLS), BF16),
-            pltpu.VMEM((ROUNDS, 2, X, 2 * RB, OUT_COLS), BF16),
-            pltpu.VMEM((ROUNDS, 2 * RB, OUT_COLS), BF16),
-            pltpu.VMEM((ROUNDS, 2 * RB, OUT_COLS), BF16),
-            pltpu.VMEM((ROUNDS, Z, 2 * RB, OUT_COLS), BF16),
-            pltpu.VMEM((ROUNDS, 2 * X, 2 * RB, OUT_COLS), BF16),
+            pltpu.VMEM((ROUNDS, Z, 2 * RB, 2 * OUT_COLS), BF16),
+            pltpu.VMEM((ROUNDS, X, 2, 2 * RB, 2 * OUT_COLS), BF16),
+            pltpu.VMEM((ROUNDS, 3, 2 * RB, OUT_COLS), BF16),
+            pltpu.VMEM((ROUNDS, 3, 2 * RB, OUT_COLS), BF16),
             dma((9,)),
             *[dma((ROUNDS,))] * 6,
             *[dma((5,))] * 2,
-            dma((ROUNDS, Z, 5)),
+            dma((ROUNDS,)),
             dma((ROUNDS, Z)),
-            dma((ROUNDS, Z, 2)),
-            dma((ROUNDS, Z)),
-            dma((ROUNDS, 2, X)),
-            *[dma((ROUNDS,))] * 2,
-            *[dma((ROUNDS, Z, 2))] * 2,
+            dma((ROUNDS,)),
+            dma((ROUNDS, 2)),
+            *[dma((ROUNDS, 3))] * 2,
+            *[dma((ROUNDS, 3))] * 2,
         ],
         compiler_params=pltpu.CompilerParams(
             collective_id=bit + 1, has_side_effects=True, vmem_limit_bytes=48 << 20

time: 60.5 us -> 64.7 us (1.069); the launches traced: 60.4 us -> 63.8 us
  Pallas kernels: 58.8 us -> 62.2 us
    pallas_call x1, Pallas kernels: 58.8 us -> 62.2 us  [attention(): pl.pallas_call(functools.partial(kernel, bit), name=f'attention_{bit}', o...]
where the time goes in v1:
time: 64.7 us; the launch traced here: 63.8 us
  Pallas kernels  62.2 us (96%)
  local copies, waits for them, and re-layouts  0.68 us (1%)
  between operations  0.66 us (1%)
    pallas_call x1, Pallas kernels, attention(): pl.pallas_call(functools.partial(kernel, bit), name=f'attention_{bit}', o...  62.2 us

profile of v1, /device:TPU:1, one launch (start us, length us, event | category | flops | bytes accessed | tf_op | source)
XLA Modules:
  0.0 63.8 jit_solution(6830907099881085944)
XLA Ops:
  0.7 62.5 %conditional.1 = (bf16[256,384]{1,0:T(8,128)(2,1)S(1)}) conditional(s32[]{:T(128)} %bitcast.55, (s32[512]{0:T(512)}, bf16[16,12,4,128]{3,2,1,0:T(4,128)(2,1)}, bf16[16,4,128]{2,1,0:T(4,128)(2,1)}, bf16[16,4,128]{2,1,0:T(4,128)(2,1)}, bf16[16,1,128,128]{3,2,1,0:T(8,128)(2,1)}, ...), branch_computations={%region_0.0_spmd, %region_1.0_spmd, %region_2.0_spmd, %region_3.0_... | conditional | bytes 8 | solution.py:456
  0.7 62.2 %attention_1.1 = bf16[256,384]{1,0:T(8,128)(2,1)S(1)} custom-call(s32[512]{0:T(512)} %get-tuple-element.193.lengths_hbm, bf16[4,192,128]{2,1,0:T(8,128)(2,1)} %bitcast.86, bf16[4,16,128]{2,1,0:T(8,128)(2,1)} %bitcast.91, bf16[4,16,128]{2,1,0:T(8,128)(2,1)} %bitcast.96, bf16[16,128,128]{2,1,0:T(8,128)(2,1)} %bitcast.61, bf16[16,128,128]{2,1,0:T(8,128)(2,1)} %bitcast.66, ...), custom_call_target="tpu_custom_call" | custom-call | tf_op jit(solution)/shard_map/cond/branch_1_fun/attention_1/pallas_call | solution.py:400
  63.1 0.7 %copy.82 = bf16[256,384]{1,0:T(8,128)(2,1)} copy(bf16[256,384]{1,0:T(8,128)(2,1)S(1)} %get-tuple-element.146) | data formatting | bytes 393216
